TPU v7x, 512 devices: a whole 4x4x16 slice. The times are simulated.
512 devices in a mesh: row: 16 (over z_lo, x), col: 32 (over z_hi, y, core).
Axes of the slice: x: 4, y: 4, z: 16 (z_hi: 4, z_lo: 4; z = z_hi * 4 + z_lo), core: 2. Of those that a mesh axis runs over, the one named last changes fastest.
Arguments:
- b_diag: float32 [512, 512], P('row'), as said below
- a_diag: float32 [512, 512], P('row'), as said below
- b_panel: float32 [16384, 512], P(('row', 'col')), may hold values from -2 to 2
- a_panel: float32 [16384, 512], P(('row', 'col')), may hold values from -2 to 2
- a_trail: float32 [16384, 16384], P('row', 'col'), as said below
Outputs:
- a_diag_new: float32 [512, 512], P('row')
- l_panel: float32 [16384, 512], P(('row', 'col'))
- a_panel_new: float32 [16384, 512], P(('row', 'col'))
- a_trail_new: float32 [16384, 16384], P('row', 'col')
Inputs may be any that keep to these rules, and one draw needn't show every extreme that they name: b_diag is symmetric positive definite, its smallest eigenvalue 0.5 or more. a_diag is symmetric. a_trail is symmetric.
All inputs are finite; a program needn't handle non-finite values.
Results may differ from a plain program's by a relative error of at most 0.0001.
Values sent between devices are 32-bit elements; how exact they have to be, the bound alone decides.
A program may use at most 64 MiB of HBM per device.

v0:
```python
import jax
import jax.numpy as jnp
from jax import lax
from jax.sharding import Mesh
from jax.sharding import PartitionSpec as P

ROW = ("row_0", "row_1")
ROW_COL = ("row_0", "row_1", "col")


HIGHEST = lax.Precision.HIGHEST


def in_order(pieces, dim):
    pieces = jnp.moveaxis(pieces, 0, dim)
    lengths = pieces.shape
    return pieces.reshape(*lengths[:dim], lengths[dim] * lengths[dim + 1], *lengths[dim + 2 :])


def from_everyone(array, axis):
    copies = jnp.broadcast_to(array, (lax.axis_size(axis), *array.shape))
    return lax.all_to_all(copies, axis, split_axis=0, concat_axis=0, tiled=True)


def gathered_copies(array, axis, dim):
    return in_order(from_everyone(array, axis), dim)


def gather_in_order(array, axes, order):
    pieces = array[None]
    for k in order:
        pieces = lax.all_gather(pieces, axes[k], axis=0, tiled=True)
    block = [lax.axis_size(axes[k]) for k in reversed(order)]
    pieces = pieces.reshape(*block, *array.shape)
    turned = sorted(range(len(order)), key=lambda place: order[len(order) - 1 - place])
    return pieces.transpose(*turned, *range(len(order), pieces.ndim)).reshape(-1, *array.shape)


def gather_axes(array, axes, order, dim):
    return in_order(gather_in_order(array, axes, order), dim)


def sent_together(arrays, axis, dim, along):
    ends, at = ([], 0)
    for a in arrays[:-1]:
        at += a.shape[along]
        ends.append(at)
    both = jnp.concatenate(arrays, axis=along)
    return tuple(jnp.split(lax.all_gather(both, axis, axis=dim, tiled=True), ends, axis=along))


def spread(array, axis, root):
    mine = lax.axis_index(axis) == root
    return lax.psum(jnp.where(mine, array, jnp.zeros_like(array)), axis)


def matmul(left, right):
    return jnp.dot(left, right, precision=HIGHEST, preferred_element_type=jnp.float32)


def outer_sum(left, right):
    return lax.dot_general(
        left, right, (((1,), (1,)), ((), ())), precision=HIGHEST, preferred_element_type=jnp.float32
    )


def invert_factor(b_full):
    factor = jnp.linalg.cholesky(b_full)
    identity = jnp.eye(b_full.shape[0], dtype=b_full.dtype)
    return jax.scipy.linalg.solve_triangular(factor, identity, lower=True)


def shards(b_diag, a_diag, b_panel, a_panel, a_trail):
    piece_rows = a_diag.shape[0]
    b_full = gathered_copies(b_diag, ROW, 0)
    inverse = invert_factor(b_full)
    right_piece = matmul(a_diag, inverse.T)
    right_full = gather_axes(right_piece, ROW, (0, 1), 0)
    a_diag_full = matmul(inverse, right_full)
    grid_row = lax.axis_index(ROW)
    a_diag_new = lax.dynamic_slice_in_dim(a_diag_full, grid_row * piece_rows, piece_rows, 0)
    l_panel = matmul(b_panel, inverse.T)
    correction = 0.5 * matmul(l_panel, a_diag_full)
    mixed = matmul(a_panel, inverse.T) - correction
    a_panel_new = mixed - correction
    row_factor, row_mixed = sent_together((l_panel, mixed), "col", 0, 1)
    height = a_trail.shape[0]
    width_cols = a_trail.shape[1]
    grid_col = lax.axis_index("col")
    source_row = grid_col * width_cols // height
    start = jnp.clip(grid_col * width_cols - grid_row * height, 0, height - width_cols)
    outgoing = (
        lax.dynamic_slice_in_dim(row_factor, start, width_cols, 0),
        lax.dynamic_slice_in_dim(row_mixed, start, width_cols, 0),
    )
    col_factor, col_mixed = (
        spread(outgoing[0], ROW, source_row),
        spread(outgoing[1], ROW, source_row),
    )
    a_trail_new = a_trail - outer_sum(row_mixed, col_factor) - outer_sum(row_factor, col_mixed)
    return (a_diag_new, l_panel, a_panel_new, a_trail_new)


def solution(mesh):
    split = Mesh(mesh.devices.reshape(4, 4, mesh.shape["col"]), ("row_0", "row_1", "col"))
    return jax.shard_map(
        shards,
        mesh=split,
        in_specs=(P(ROW, None), P(ROW, None), P(ROW_COL, None), P(ROW_COL, None), P(ROW, "col")),
        out_specs=(P(ROW, None), P(ROW_COL, None), P(ROW_COL, None), P(ROW, "col")),
        check_vma=False,
    )
```

profile of v0, /device:TPU:24, one launch (start us, length us, event | category | flops | bytes accessed | tf_op | source)
XLA Modules:
  0.0 532.8 jit_solution(2031386575050240520)
XLA Ops:
  7.2 2.0 broadcast_in_dim.8
  9.1 8.5 %all-to-all-start = ((f32[16,32,512]{2,1,0:T(8,128)}), f32[16,32,512]{2,1,0:T(8,128)S(1)}, u32[]{:S(2)}, u32[]{:S(2)}) async-start(f32[16,32,512]{2,1,0:T(8,128)} %broadcast_in_dim.8), calls=%async_computation | async-start | bytes 2097152 | tf_op jit(solution)/shard_map/all_to_all | solution.py:22
  17.9 24.3 %all-to-all-done = f32[16,32,512]{2,1,0:T(8,128)S(1)} async-done(((f32[16,32,512]{2,1,0:T(8,128)}), f32[16,32,512]{2,1,0:T(8,128)S(1)}, u32[]{:S(2)}, u32[]{:S(2)}) %all-to-all-start) | async-done | bytes 1048608 | tf_op jit(solution)/shard_map/all_to_all | solution.py:22
  43.8 11.7 %cholesky.104 = f32[128,128]{1,0:T(8,128)S(1)} custom-call(f32[128,128]{1,0:T(8,128)S(1)} %cholesky.266), custom_call_target="Cholesky" | custom-call | tf_op jit(solution)/shard_map/jit(cholesky)/cholesky | solution.py:68
  55.6 9.8 %custom-call.31 = f32[1,128,128]{1,2,0:T(8,128)S(1)} custom-call(f32[1,128,128]{2,1,0:T(8,128)S(1)} %get-tuple-element.35), custom_call_target="InvertDiagBlocksLowerTriangular" | custom-call | tf_op jit(solution)/shard_map/jit(cholesky)/cholesky | solution.py:68
  65.5 1.2 constant_dynamic-update-slice_fusion.1
  66.7 1.3 convolution_subtract_fusion.3
  68.0 11.7 %cholesky.217 = f32[128,128]{1,0:T(8,128)S(1)} custom-call(f32[128,128]{1,0:T(8,128)S(1)} %cholesky.270), custom_call_target="Cholesky" | custom-call | tf_op jit(solution)/shard_map/jit(cholesky)/cholesky | solution.py:68
  79.8 10.3 %custom-call.32 = f32[1,128,128]{1,2,0:T(8,128)S(1)} custom-call(f32[1,128,128]{2,1,0:T(8,128)S(1)} %get-tuple-element.32), custom_call_target="InvertDiagBlocksLowerTriangular" | custom-call | tf_op jit(solution)/shard_map/jit(cholesky)/cholesky | solution.py:68
  90.3 1.3 convolution_subtract_fusion.4
  91.6 11.7 %cholesky.238 = f32[128,128]{1,0:T(8,128)S(1)} custom-call(f32[128,128]{1,0:T(8,128)S(1)} %cholesky.275), custom_call_target="Cholesky" | custom-call | tf_op jit(solution)/shard_map/jit(cholesky)/cholesky | solution.py:68
  104.0 9.8 %custom-call.33 = f32[1,128,128]{1,2,0:T(8,128)S(1)} custom-call(f32[1,128,128]{2,1,0:T(8,128)S(1)} %get-tuple-element.29), custom_call_target="InvertDiagBlocksLowerTriangular" | custom-call | tf_op jit(solution)/shard_map/jit(cholesky)/cholesky | solution.py:68
  114.0 1.2 convolution_subtract_fusion.5
  115.3 11.7 %cholesky.255 = f32[128,128]{1,0:T(8,128)S(1)} custom-call(f32[128,128]{1,0:T(8,128)S(1)} %convolution_subtract_fusion.5), custom_call_target="Cholesky" | custom-call | tf_op jit(solution)/shard_map/jit(cholesky)/cholesky | solution.py:68
  131.2 10.4 %while.1 = (s32[]{:T(128)}, f32[512,512]{1,0:T(8,128)S(1)}, s32[4,2]{0,1:T(2,128)S(1)}, f32[4,128,128]{2,1,0:T(8,128)}, s32[]{:T(128)}) while((s32[]{:T(128)}, f32[512,512]{1,0:T(8,128)S(1)}, s32[4,2]{0,1:T(2,128)S(1)}, f32[4,128,128]{2,1,0:T(8,128)}, s32[]{:T(128)}) %tuple.33), condition=%wide.while_cond, body=%wide.while_body.sunk | while | flops 2 | bytes 132205 | solution.py:70
  131.8 2.0 bitcast_dynamic-update-slice_fusion.2
  134.4 2.0 bitcast_dynamic-update-slice_fusion.2
  137.0 2.0 bitcast_dynamic-update-slice_fusion.2
  139.6 2.0 bitcast_dynamic-update-slice_fusion.2
  141.6 40.1 %custom-call.34 = f32[4,128,128]{1,2,0:T(8,128)S(1)} custom-call(f32[4,128,128]{2,1,0:T(8,128)} %get-tuple-element.11), custom_call_target="InvertDiagBlocksLowerTriangular" | custom-call | tf_op jit(solution)/shard_map/jit(_solve_triangular)/triangular_solve | solution.py:70
  184.4 1.3 fusion.21
  186.7 16.5 %all-gather = f32[128,512]{1,0:T(8,128)} all-gather(f32[32,512]{1,0:T(8,128)S(1)} %convolution_bitcast_fusion.1), channel_id=2, replica_groups=mesh['row_0'=4,'row_1'=4,'col'=32] {'row_0'}, dimensions={0}, use_global_device_ids=true | all-gather | bytes 327680 | tf_op jit(solution)/shard_map/all_gather | solution.py:32
  204.5 30.2 %all-gather.4.cloned.1.call-done = f32[16,32,512]{2,1,0:T(8,128)} async-done(((f32[4,32,512]{2,1,0:T(8,128)}), f32[16,32,512]{2,1,0:T(8,128)}) %all-gather.4.cloned.1.call-update) | async-done | bytes 1048592 | tf_op jit(solution)/shard_map/all_gather | solution.py:32
  234.7 1.3 copy.15
  236.0 1.9 fusion.36
  238.6 1.7 fusion.39
  241.3 95.3 %all-gather.6.cloned.1.call-done = f32[1024,1024]{1,0:T(8,128)} async-done(((f32[32,1024]{1,0:T(8,128)}), f32[1024,1024]{1,0:T(8,128)}) %all-gather.6.cloned.1.call-update) | async-done | bytes 4194320 | tf_op jit(solution)/shard_map/all_gather | solution.py:49
  336.6 2.7 fusion.38
  339.3 1.2 dynamic-slice_select_fusion
  342.2 173.4 %all-reduce.4.cloned.1.call-done = (f32[512,512]{1,0:T(8,128)}, f32[512,512]{1,0:T(8,128)}) async-done(((f32[512,512]{1,0:T(8,128)}, f32[512,512]{1,0:T(8,128)}), (f32[512,512]{1,0:T(8,128)}, f32[512,512]{1,0:T(8,128)})) %all-reduce.4.cloned.1.call-update) | async-done | bytes 2097168 | tf_op jit(solution)/shard_map/psum | solution.py:54
  515.6 5.5 %fusion.33 = f32[1024,512]{1,0:T(8,128)S(1)} fusion(f32[512,512]{1,0:T(8,128)} %get-tuple-element.20, f32[1024,1024]{1,0:T(8,128)} %all-gather.6.cloned.1.call-done), kind=kOutput, calls=%fused_computation.78 | convolution fusion | flops 3221225472 | bytes 5242880 | tf_op jit(solution)/shard_map/dot_general | solution.py:62
  521.1 5.0 subtract_subtract_fusion
  (65 shorter events, 15.3 us)
Async XLA Ops:
  7.2 231.4 %copy-start = (f32[32,512]{1,0:T(8,128)S(1)}, f32[32,512]{1,0:T(8,128)}, u32[]{:S(2)}) copy-start(f32[32,512]{1,0:T(8,128)} %param.8) | copy-start | bytes 196612
  9.1 33.1 %all-to-all-start = ((f32[16,32,512]{2,1,0:T(8,128)}), f32[16,32,512]{2,1,0:T(8,128)S(1)}, u32[]{:S(2)}, u32[]{:S(2)}) async-start(f32[16,32,512]{2,1,0:T(8,128)} %broadcast_in_dim.8), calls=%async_computation | async-start | bytes 2097152 | tf_op jit(solution)/shard_map/all_to_all | solution.py:22
  17.6 217.1 %all-gather.4.cloned.1.call-start = ((), (), s32[]{:S(2)}) async-start(), calls=%async_computation.1 | async-start | bytes 1310720 | tf_op jit(solution)/shard_map/all_gather | solution.py:32
  42.8 1.0 copy-start.2
  181.7 1.6 copy-start.5
  182.4 3.2 copy-start.7
  183.7 19.6 %copy-start.8 = (f32[32,512]{1,0:T(8,128)S(1)}, f32[32,512]{1,0:T(8,128)}, u32[]{:S(2)}) copy-start(f32[32,512]{1,0:T(8,128)} %param.7) | copy-start | bytes 196612
  203.3 133.3 %all-gather.6.cloned.1.call-start = ((), (), s32[]{:S(2)}) async-start(), calls=%async_computation.2 | async-start | bytes 4325376 | tf_op jit(solution)/shard_map/all_gather | solution.py:49
  204.4 35.9 %copy-start.6 = (f32[512,32]{0,1:T(8,128)}, f32[512,32]{0,1:T(8,128)S(1)}, u32[]{:S(2)}) copy-start(f32[512,32]{0,1:T(8,128)S(1)} %fusion.35) | copy-start | bytes 196612
  241.0 274.6 %all-reduce.4.cloned.1.call-start = ((), (), s32[]{:S(2)}) async-start(), calls=%async_computation.3 | async-start | bytes 4194304 | tf_op jit(solution)/shard_map/psum | solution.py:54
  341.5 179.5 %copy-start.3 = (f32[1024,512]{1,0:T(8,128)S(1)}, f32[1024,512]{1,0:T(8,128)}, u32[]{:S(2)}) copy-start(f32[1024,512]{1,0:T(8,128)} %param.9) | copy-start | bytes 6291460
  515.6 5.5 %copy-start.1 = (f32[1024,1024]{1,0:T(8,128)S(1)}, f32[1024,1024]{1,0:T(8,128)}, u32[]{:S(2)}) copy-start(f32[1024,1024]{1,0:T(8,128)} %all-gather.6.cloned.1.call-done) | copy-start | bytes 12582916
  515.6 5.5 %copy-start.4 = (f32[512,512]{1,0:T(8,128)S(1)}, f32[512,512]{1,0:T(8,128)}, u32[]{:S(2)}) copy-start(f32[512,512]{1,0:T(8,128)} %get-tuple-element.21) | copy-start | bytes 3145732
Sparse Core Ops, SparseCore 0:
  203.4 31.2 all-gather.3
  241.1 95.4 all-gather.5
  341.7 173.8 all-reduce.3
where the time goes:
time: 542 us; the launch traced here: 533 us
  waiting for transfers between devices  323 us (60%)
  other arithmetic  123 us (23%)
  matrix products  26.2 us (5%)
  local copies, waits for them, and re-layouts  18.5 us (3%)
  between operations  17 us (3%)
  blocking collectives  16.5 us (3%)
  starting transfers between devices  8.8 us (2%)
    psum x1, waiting for transfers between devices, spread(): return lax.psum(jnp.where(mine, array, jnp.zeros_like(array)), axis)  173 us
    all_gather x1, waiting for transfers between devices, sent_together(): lax.all_gather(both, axis, axis=dim, tiled=True)  95.3 us
    another operation x14, other arithmetic, invert_factor(): factor = jnp.linalg.cholesky(b_full)  78.9 us
    another operation x3, other arithmetic, invert_factor(): return jax.scipy.linalg.solve_triangular(factor, identity, lower=True)  40.3 us
    all_gather x1, waiting for transfers between devices, gather_in_order(): pieces = lax.all_gather(pieces, axes[k], axis=0, tiled=True)  30.2 us
    all_to_all x1, waiting for transfers between devices, from_everyone(): return lax.all_to_all(copies, axis, split_axis=0, concat_axis=0, tiled=True)  24.3 us
    all_gather x1, blocking collectives, gather_in_order(): pieces = lax.all_gather(pieces, axes[k], axis=0, tiled=True)  16.5 us
  transfers between devices with their start and end apart: 4, of which 4 were waited for; matrix products, arithmetic and copies ran while one was open for 0% of the time, Pallas kernels for 0%

commit v1 on v0

v1 whole, which is shorter than its diff:
```python
import functools

import jax
import jax.numpy as jnp
from jax import lax
from jax.experimental import pallas as pl
from jax.experimental.pallas import tpu as pltpu
from jax.sharding import Mesh
from jax.sharding import PartitionSpec as P

f32 = jnp.float32
bf16 = jnp.bfloat16
MESH = pl.DeviceIdType.MESH
HIGHEST = lax.Precision.HIGHEST
NN = ((1,), (0,))
NT = ((1,), (1,))


def dot(a, b, dims):
    return lax.dot_general(a, b, (dims, ((), ())), precision=HIGHEST, preferred_element_type=f32)


def halves(x):
    hi = x.astype(bf16)
    return hi, (x - hi.astype(f32)).astype(bf16)


def dot3(a, b, dims):
    def one(u, v):
        return lax.dot_general(u, v, (dims, ((), ())), preferred_element_type=f32)

    return one(a[0], b[0]) + (one(a[0], b[1]) + one(a[1], b[0]))


def lane_bcast(x, j):
    return jnp.broadcast_to(x[:, j : j + 1], (8, 128))


def sub_bcast(x, k):
    return jnp.broadcast_to(x[k : k + 1, :], (8, 128))


def base64(block, odd):
    lane = lax.broadcasted_iota(jnp.int32, (8, 128), 1)
    sub = lax.broadcasted_iota(jnp.int32, (8, 128), 0)
    to, at = 64 * odd, 64 - 64 * odd
    mine = (lane >= 64) if odd else (lane < 64)
    turned = pltpu.roll(block, 64, 1)
    rows_of = []
    for g in range(8):
        eye = jnp.where(lane == sub + (8 * g + to), 1.0, 0.0).astype(f32)
        rows_of.append(jnp.where(mine, eye, turned[8 * g : 8 * g + 8, :]))
    out = []
    for g in range(8):
        rows = rows_of[g]
        cols = [lane_bcast(rows, at + 8 * g + k) for k in range(8)]
        done = jnp.zeros((8, 128), f32)
        for k in range(8):
            is_k = sub == k
            row = sub_bcast(rows, k)
            pivot = sub_bcast(cols[k], k)
            inv = 1.0 / pivot
            done = jnp.where(is_k, row * lax.rsqrt(pivot), done)
            m = cols[k] * inv
            rows = jnp.where(is_k, row * inv, rows - m * row)
            for j in range(k + 1, 8):
                top = sub_bcast(cols[j], k)
                cols[j] = jnp.where(is_k, top * inv, cols[j] - m * top)
        out.append(jnp.where(mine, done, 0.0))
        if g < 7:
            tops = [sub_bcast(rows, k) for k in range(8)]
            for i in range(g + 1, 8):
                t = [lane_bcast(rows_of[i], at + 8 * g + k) * tops[k] for k in range(8)]
                rows_of[i] = rows_of[i] - (((t[0] + t[1]) + (t[2] + t[3])) + ((t[4] + t[5]) + (t[6] + t[7])))
    return jnp.concatenate(out, axis=0)


def invert(aw, between):
    following = None
    for k in range(8):
        odd = k % 2
        w0, r0 = 64 * (k - odd), 64 * k
        own = base64(aw[r0 : r0 + 64, w0 : w0 + 128], odd) if k == 0 else following
        c0 = 64 * (k + 1) if odd else 64 * k
        c1 = 512 + 64 * (k + 1) if odd else 512 + 64 * (k + 2)
        if k < 7:
            odd_next = (k + 1) % 2
            n0 = 64 * (k + 1 - odd_next)
            left = dot(aw[r0 + 64 : r0 + 128, w0 : w0 + 128], own, NT)
            right = dot(own, aw[w0 : w0 + 128, n0 : n0 + 128], NN)
            following = base64(aw[r0 + 64 : r0 + 128, n0 : n0 + 128] - dot(left, right, NN), odd_next)
        right = dot(own, aw[w0 : w0 + 128, c0:c1], NN)
        if k < 7:
            left = dot(aw[r0 + 64 : 512, w0 : w0 + 128], own, NT)
            aw[r0 + 64 : 512, c0:c1] = aw[r0 + 64 : 512, c0:c1] - dot(left, right, NN)
        aw[r0 : r0 + 64, 512:c1] = right[:, 512 - c0 :]
        between(k)


class Copies:
    def __init__(self, send, recv):
        self.send, self.recv, self.sent = send, recv, []

    def describe(self, n, src, dst, dev):
        return pltpu.make_async_remote_copy(
            src_ref=src, dst_ref=dst, send_sem=self.send.at[n], recv_sem=self.recv.at[n], device_id=dev, device_id_type=MESH
        )

    def start(self, n, src, dst, dev):
        copy = self.describe(n, src, dst, dev)
        copy.start()
        self.sent.append(copy)

    def arrived(self, n, dst, dev):
        self.describe(n, dst, dst, dev).wait_recv()

    def finish(self):
        for copy in self.sent:
            copy.wait_send()


def kernel(
    b_diag, a_diag, b_panel, a_panel, a_trail,
    diag_out, l_out, n_out, trail_out,
    aw, bd, ad, pr, pc, st, adn, mid, trail, zh, zl,
    send, recv, local, tin, tout,
):
    zlo, x, zhi, y, core = (lax.axis_index(a) for a in ("z_lo", "x", "z_hi", "y", "core"))
    grid_row = zlo * 4 + x
    other = 1 - core

    def up(i, d):
        return lax.rem(i + d, 4)

    load_trail = pltpu.make_async_copy(a_trail, trail, tin.at[0])

    def place(zh_, y_, c_):
        return pl.ds(pl.multiple_of((zh_ * 8 + y_ * 2 + c_) * 32, 32), 32)

    own = place(zhi, y, core)
    own_b = pltpu.make_async_copy(b_panel, pr.at[own, pl.ds(0, 512)], local.at[0])
    own_a = pltpu.make_async_copy(a_panel, pr.at[own, pl.ds(512, 512)], local.at[1])
    half = pl.ds(pl.multiple_of(core * 16, 16), 16)
    own_bd = pltpu.make_async_copy(b_diag.at[half], bd.at[zlo, x, core], local.at[2])
    own_ad = pltpu.make_async_copy(a_diag.at[half], ad.at[zlo, x, core], local.at[3])
    own_bd.start()
    own_b.start()
    own_a.start()
    own_ad.start()

    peers = []
    peers += [{"z_lo": up(zlo, d)} for d in (1, 2, 3)]
    peers += [{"x": up(x, d), "core": c} for d in (1, 3) for c in (0, 1)]
    peers += [{"z_hi": up(zhi, d)} for d in (1, 3)]
    peers += [{"y": up(y, d)} for d in (1, 3)]
    peers += [{"core": other}]
    turned = {"z_lo": zhi, "x": y, "z_hi": zlo, "y": x}
    stays = jnp.logical_and(zlo == zhi, x == y)
    barrier = pltpu.get_barrier_semaphore()
    for dev in peers:
        pl.semaphore_signal(barrier, inc=1, device_id=dev, device_id_type=MESH)

    @pl.when(jnp.logical_not(stays))
    def _():
        pl.semaphore_signal(barrier, inc=1, device_id=turned, device_id_type=MESH)

    pl.semaphore_wait(barrier, len(peers) + 1 - stays.astype(jnp.int32))

    copies = Copies(send, recv)
    X = {1: {"x": up(x, 1)}, -1: {"x": up(x, 3)}}
    Y = {1: {"y": up(y, 1)}, -1: {"y": up(y, 3)}}
    Z = {1: {"z_hi": up(zhi, 1)}, -1: {"z_hi": up(zhi, 3)}}
    CORE = {"core": other}

    def diag_z(base, buf):
        for d in (1, 2, 3):
            copies.start(base + d - 1, buf.at[zlo, x, core], buf.at[zlo, x, core], {"z_lo": up(zlo, d)})

    def diag_x(base, buf):
        for d in (1, 2, 3):
            copies.arrived(base + d - 1, buf.at[up(zlo, 4 - d), x, core], {"z_lo": up(zlo, d)})
        mine = buf.at[:, x, core]
        copies.start(base + 3, mine, mine, X[1])
        copies.start(base + 4, mine, mine, X[-1])
        copies.start(base + 5, mine, mine, CORE)

    def diag_forward(base, buf):
        left, right = up(x, 3), up(x, 1)
        copies.arrived(base + 3, buf.at[:, left, core], X[1])
        part = buf.at[pl.ds(0, 2), left, core]
        copies.start(base + 6, part, part, X[1])
        copies.start(base + 8, buf.at[:, left, core], buf.at[:, left, core], CORE)
        copies.arrived(base + 4, buf.at[:, right, core], X[-1])
        part = buf.at[pl.ds(2, 2), right, core]
        copies.start(base + 7, part, part, X[-1])
        copies.start(base + 9, buf.at[:, right, core], buf.at[:, right, core], CORE)

    def diag_last(base, buf):
        far = up(x, 2)
        copies.arrived(base + 6, buf.at[pl.ds(0, 2), far, core], X[1])
        copies.arrived(base + 7, buf.at[pl.ds(2, 2), far, core], X[-1])
        copies.start(base + 10, buf.at[:, far, core], buf.at[:, far, core], CORE)

    def diag_end(base, buf):
        for n, place_x in ((5, x), (8, up(x, 3)), (9, up(x, 1)), (10, up(x, 2))):
            copies.arrived(base + n, buf.at[:, place_x, other], CORE)

    BD, AD = 0, 11

    ROWZ, ROWY, ROWC = 22, 26, 38
    offsets = (0, 3, 1, 2)

    def piece(o, dy, c):
        return pr.at[place(up(zhi, offsets[o]), up(y, dy), c)]

    def part_of(o, dy, c, h):
        start = (up(zhi, offsets[o]) * 8 + up(y, dy) * 2 + c) * 32 + 16 * h
        return pr.at[pl.ds(pl.multiple_of(start, 16), 16)]

    def rows_z():
        copies.start(ROWZ, piece(0, 0, core), piece(0, 0, core), Z[1])
        copies.start(ROWZ + 1, piece(0, 0, core), piece(0, 0, core), Z[-1])

    def rows_z_forward():
        copies.arrived(ROWZ, piece(1, 0, core), Z[1])
        copies.start(ROWZ + 2, part_of(1, 0, core, 0), part_of(1, 0, core, 0), Z[1])
        copies.arrived(ROWZ + 1, piece(2, 0, core), Z[-1])
        copies.start(ROWZ + 3, part_of(2, 0, core, 1), part_of(2, 0, core, 1), Z[-1])

    def rows_z_last():
        copies.arrived(ROWZ + 2, part_of(3, 0, core, 0), Z[1])
        copies.arrived(ROWZ + 3, part_of(3, 0, core, 1), Z[-1])

    def rows_y(o):
        p = piece(o, 0, core)
        copies.start(ROWY + 3 * o, p, p, Y[1])
        copies.start(ROWY + 3 * o + 1, p, p, Y[-1])
        copies.start(ROWC + 4 * o, p, p, CORE)

    def rows_y_forward(o):
        copies.arrived(ROWY + 3 * o, piece(o, 3, core), Y[1])
        if o < 2:
            copies.start(ROWY + 3 * o + 2, piece(o, 3, core), piece(o, 3, core), Y[1])
        copies.arrived(ROWY + 3 * o + 1, piece(o, 1, core), Y[-1])
        if o >= 2:
            copies.start(ROWY + 3 * o + 2, piece(o, 1, core), piece(o, 1, core), Y[-1])
        copies.start(ROWC + 4 * o + 1, piece(o, 3, core), piece(o, 3, core), CORE)
        copies.start(ROWC + 4 * o + 2, piece(o, 1, core), piece(o, 1, core), CORE)

    def rows_y_last(o):
        copies.arrived(ROWY + 3 * o + 2, piece(o, 2, core), Y[1] if o < 2 else Y[-1])
        copies.start(ROWC + 4 * o + 3, piece(o, 2, core), piece(o, 2, core), CORE)

    def rows_end():
        for o in range(4):
            for n, dy in ((0, 0), (1, 3), (2, 1), (3, 2)):
                copies.arrived(ROWC + 4 * o + n, piece(o, dy, other), CORE)

    TURN, COLZ, COLX = 54, 55, 58

    def turn():
        @pl.when(stays)
        def _():
            pltpu.make_async_copy(pr.at[own], st.at[zhi], recv.at[TURN]).start()

        @pl.when(jnp.logical_not(stays))
        def _():
            copies.describe(TURN, pr.at[own], st.at[zhi], turned).start()

    def turned_here():
        @pl.when(stays)
        def _():
            pltpu.make_async_copy(pr.at[own], st.at[zhi], recv.at[TURN]).wait()

        @pl.when(jnp.logical_not(stays))
        def _():
            copies.arrived(TURN, st.at[zlo], turned)

    def turn_sent():
        @pl.when(jnp.logical_not(stays))
        def _():
            copies.describe(TURN, pr.at[own], st.at[zhi], turned).wait_send()

    def cols_z():
        for d in (1, 2, 3):
            copies.start(COLZ + d - 1, st.at[zlo], st.at[zlo], {"z_lo": up(zlo, d)})

    def cols_z_end():
        for d in (1, 2, 3):
            copies.arrived(COLZ + d - 1, st.at[up(zlo, 4 - d)], {"z_lo": up(zlo, d)})

    def spot(i, v, s):
        return pc.at[pl.ds(pl.multiple_of((i * 8 + v * 2 + s) * 32, 32), 32)]

    def col_copy(way, h, s, dev):
        n = COLX + 4 * way + 2 * (h % 2)
        return pltpu.make_async_remote_copy(
            src_ref=st.at[h], dst_ref=spot(h % 2, x, s), send_sem=send.at[COLX + 4 * way + h],
            recv_sem=recv.at[n + s], device_id=dev, device_id_type=MESH,
        )

    def on_core(s, h, there):
        n = COLX + 8 + 2 * (h % 2) + s
        if h // 2 == s:
            return pltpu.make_async_copy(st.at[h], spot(h % 2, x, s), recv.at[n])
        return col_copy(2, h, s, {"core": 1 - s})

    def cols_x():
        for s in (0, 1):

            @pl.when(core == s)
            def _(s=s):
                for h in range(4):
                    for way, dx in ((0, 1), (1, 3)):
                        col_copy(way, h, s, {"x": up(x, dx), "core": h // 2}).start()
                    on_core(s, h, None).start()

    def cols_x_sent():
        for s in (0, 1):

            @pl.when(core == s)
            def _(s=s):
                for h in range(4):
                    for way, dx in ((0, 1), (1, 3)):
                        col_copy(way, h, s, {"x": up(x, dx), "core": h // 2}).wait_send()
                    if h // 2 != s:
                        on_core(s, h, None).wait_send()

    FAR = COLX + 16

    def cols_forward():
        for i in (0, 1):
            for s in (0, 1):
                copies.arrived(COLX + 2 * i + s, spot(i, up(x, 3), s), X[1])
                copies.arrived(COLX + 4 + 2 * i + s, spot(i, up(x, 1), s), X[-1])
            p = spot(i, up(x, 3), 0)
            copies.start(FAR + 2 * i, p, p, X[1])
            p = spot(i, up(x, 1), 1)
            copies.start(FAR + 2 * i + 1, p, p, X[-1])

    def cols_end():
        for i in (0, 1):
            for s in (0, 1):
                copies.arrived(COLX + 8 + 2 * i + s, spot(i, x, s), CORE)
                copies.arrived(FAR + 2 * i + s, spot(i, up(x, 2), s), X[1])

    own_bd.wait()
    diag_z(BD, bd)
    own_b.wait()
    own_a.wait()
    rows_z()
    turn()
    rows_y(0)
    load_trail.start()
    diag_x(BD, bd)
    own_ad.wait()
    diag_z(AD, ad)
    diag_forward(BD, bd)
    diag_last(BD, bd)
    eye = lax.broadcasted_iota(jnp.int32, (512, 512), 0) == lax.broadcasted_iota(jnp.int32, (512, 512), 1)
    aw[:, 512:] = jnp.where(eye, 1.0, 0.0).astype(f32)
    diag_end(BD, bd)
    aw[:, :512] = bd[...].reshape(512, 512)

    def between(k):
        if k == 0:
            turned_here()
            cols_z()
            rows_y_forward(0)
            diag_x(AD, ad)
        if k == 1:
            rows_z_forward()
            rows_y(1)
            rows_y(2)
        if k == 2:
            cols_z_end()
            cols_x()
            rows_y_last(0)
            diag_forward(AD, ad)
        if k == 3:
            rows_y_forward(1)
            rows_y_forward(2)
            diag_last(AD, ad)
        if k == 4:
            rows_z_last()
            rows_y(3)
        if k == 5:
            rows_y_last(1)
            rows_y_last(2)
        if k == 6:
            rows_y_forward(3)
        if k == 7:
            cols_forward()

    invert(aw, between)
    diag_end(AD, ad)
    mid[...] = dot(ad[...].reshape(512, 512), aw[:, 512:], NT)
    rows_y_last(3)
    w = halves(aw[:, 512:])
    adn[...] = dot(aw[:, 512:], mid[...], NN)
    diag_out[...] = adn[pl.ds(pl.multiple_of(grid_row * 32, 32), 32), :]
    q = halves(adn[...])
    own_l = dot3(halves(pr[own, 0:512]), w, NT)
    l_out[...] = own_l
    n_out[...] = dot3(halves(pr[own, 512:1024]), w, NT) - dot3(halves(own_l), q, NN)
    cols_end()
    col_l = dot3(halves(pc[:, 0:512]), w, NT)
    lh = halves(col_l)
    col_n = dot3(halves(pc[:, 512:1024]), w, NT) - dot3(lh, q, NN)
    col_y = dot3(lh, w, NN)
    col_z = dot3(halves(col_n), w, NN)
    zh[:, 0:512], zl[:, 0:512] = halves(col_z)
    zh[:, 512:1024], zl[:, 512:1024] = halves(col_y)
    load_trail.wait()
    rows_end()

    def store(t):
        tile = pl.ds(pl.multiple_of(t * 128, 128), 128)
        return pltpu.make_async_copy(trail.at[tile], trail_out.at[tile], tout.at[t])

    @pl.loop(0, 8)
    def _(t):
        tile = pl.ds(pl.multiple_of(t * 128, 128), 128)
        trail[tile, :] = trail[tile, :] - dot3(halves(pr[tile, :]), (zh[...], zl[...]), NT)
        store(t).start()

    copies.finish()
    turn_sent()
    cols_x_sent()
    for t in range(8):
        store(t).wait()


def shards(*arrays):
    vmem = pl.BlockSpec(memory_space=pltpu.VMEM)
    anywhere = pl.BlockSpec(memory_space=pl.ANY)
    own = jax.ShapeDtypeStruct((32, 512), f32)
    return pl.pallas_call(
        kernel,
        out_shape=(own, own, own, jax.ShapeDtypeStruct((1024, 512), f32)),
        in_specs=[anywhere] * 5,
        out_specs=(vmem, vmem, vmem, anywhere),
        scratch_shapes=[
            pltpu.VMEM((512, 1024), f32),
            pltpu.VMEM((4, 4, 2, 16, 512), f32),
            pltpu.VMEM((4, 4, 2, 16, 512), f32),
            pltpu.VMEM((1024, 1024), f32),
            pltpu.VMEM((512, 1024), f32),
            pltpu.VMEM((4, 32, 1024), f32),
            pltpu.VMEM((512, 512), f32),
            pltpu.VMEM((512, 512), f32),
            pltpu.VMEM((1024, 512), f32),
            pltpu.VMEM((512, 1024), bf16),
            pltpu.VMEM((512, 1024), bf16),
            pltpu.SemaphoreType.DMA((80,)),
            pltpu.SemaphoreType.DMA((80,)),
            pltpu.SemaphoreType.DMA((4,)),
            pltpu.SemaphoreType.DMA((1,)),
            pltpu.SemaphoreType.DMA((8,)),
        ],
        compiler_params=pltpu.CompilerParams(collective_id=0, has_side_effects=True, vmem_limit_bytes=56 << 20),
        cost_estimate=pl.CostEstimate(flops=10**10, bytes_accessed=8 << 20, transcendentals=0),
    )(*arrays)


def solution(mesh):
    names = ("z_lo", "x", "z_hi", "y", "core")
    split = Mesh(mesh.devices.reshape(4, 4, 4, 4, 2), names)
    row, col = names[:2], names[2:]
    return jax.shard_map(
        shards,
        mesh=split,
        in_specs=(P(row, None), P(row, None), P(names, None), P(names, None), P(row, col)),
        out_specs=(P(row, None), P(names, None), P(names, None), P(row, col)),
        check_vma=False,
    )
```

time: 542 us -> 116 us (0.21)
  the two profiles are of different devices: /device:TPU:24 before, /device:TPU:98 now
where the time goes in v1:
time: 116 us; the launch traced here: 115 us
  Pallas kernels  107 us (92%)
  local copies, waits for them, and re-layouts  7.5 us (6%)
    pallas_call x1, Pallas kernels, shards(): pl.pallas_call(kernel, out_shape=(own, own, own, jax.ShapeDtypeStruct((10...  107 us
    unnamed x4, local copies, waits for them, and re-layouts  7.5 us

profile of v1, /device:TPU:98, one launch (start us, length us, event | category | flops | bytes accessed | tf_op | source)
XLA Modules:
  0.0 115.4 jit_solution(7880197389141884234)
XLA Ops:
  0.6 107.3 %shard_map.84 = (f32[32,512]{1,0:T(8,128)}, f32[32,512]{1,0:T(8,128)}, f32[32,512]{1,0:T(8,128)}, f32[1024,512]{1,0:T(8,128)}) custom-call(f32[32,512]{1,0:T(8,128)} %b_diag.1, f32[32,512]{1,0:T(8,128)} %a_diag.1, f32[32,512]{1,0:T(8,128)} %b_panel.1, f32[32,512]{1,0:T(8,128)} %a_panel.1, f32[1024,512]{1,0:T(8,128)} %a_trail.1), custom_call_target="tpu_custom_call" | custom-call | flops 10000000000 | bytes 8388608 | tf_op jit(solution)/shard_map/pallas_call | solution.py:438
  107.9 1.5 %copy.13 = f32[32,512]{1,0:T(8,128)} copy(f32[32,512]{1,0:T(8,128)} %get-tuple-element.8) | data formatting | bytes 131072
  109.4 1.5 %copy.14 = f32[32,512]{1,0:T(8,128)} copy(f32[32,512]{1,0:T(8,128)} %get-tuple-element.9) | data formatting | bytes 131072
  110.9 1.5 %copy.15 = f32[32,512]{1,0:T(8,128)} copy(f32[32,512]{1,0:T(8,128)} %get-tuple-element.10) | data formatting | bytes 131072
  112.4 3.1 %copy.16 = f32[1024,512]{1,0:T(8,128)} copy(f32[1024,512]{1,0:T(8,128)} %get-tuple-element.11) | data formatting | bytes 4194304

commit v2 on v1

--- a/solution.py
+++ b/solution.py
@@ -40,7 +40,7 @@
     return jnp.broadcast_to(x[k : k + 1, :], (8, 128))
 
 
-def base64(block, odd):
+def base64(block, odd, midway):
     lane = lax.broadcasted_iota(jnp.int32, (8, 128), 1)
     sub = lax.broadcasted_iota(jnp.int32, (8, 128), 0)
     to, at = 64 * odd, 64 - 64 * odd
@@ -67,6 +67,8 @@
                 top = sub_bcast(cols[j], k)
                 cols[j] = jnp.where(is_k, top * inv, cols[j] - m * top)
         out.append(jnp.where(mine, done, 0.0))
+        if g == 3:
+            midway()
         if g < 7:
             tops = [sub_bcast(rows, k) for k in range(8)]
             for i in range(g + 1, 8):
@@ -76,11 +78,12 @@
 
 
 def invert(aw, between):
-    following = None
+    following = base64(aw[0:64, 0:128], 0, lambda: between(0))
+    between(1)
     for k in range(8):
         odd = k % 2
         w0, r0 = 64 * (k - odd), 64 * k
-        own = base64(aw[r0 : r0 + 64, w0 : w0 + 128], odd) if k == 0 else following
+        own = following
         c0 = 64 * (k + 1) if odd else 64 * k
         c1 = 512 + 64 * (k + 1) if odd else 512 + 64 * (k + 2)
         if k < 7:
@@ -88,13 +91,15 @@
             n0 = 64 * (k + 1 - odd_next)
             left = dot(aw[r0 + 64 : r0 + 128, w0 : w0 + 128], own, NT)
             right = dot(own, aw[w0 : w0 + 128, n0 : n0 + 128], NN)
-            following = base64(aw[r0 + 64 : r0 + 128, n0 : n0 + 128] - dot(left, right, NN), odd_next)
+            block = aw[r0 + 64 : r0 + 128, n0 : n0 + 128] - dot(left, right, NN)
+            following = base64(block, odd_next, lambda: between(2 * k + 2))
         right = dot(own, aw[w0 : w0 + 128, c0:c1], NN)
         if k < 7:
             left = dot(aw[r0 + 64 : 512, w0 : w0 + 128], own, NT)
             aw[r0 + 64 : 512, c0:c1] = aw[r0 + 64 : 512, c0:c1] - dot(left, right, NN)
         aw[r0 : r0 + 64, 512:c1] = right[:, 512 - c0 :]
-        between(k)
+        if k < 7:
+            between(2 * k + 3)
 
 
 class Copies:
@@ -251,10 +256,9 @@
         copies.arrived(ROWY + 3 * o + 2, piece(o, 2, core), Y[1] if o < 2 else Y[-1])
         copies.start(ROWC + 4 * o + 3, piece(o, 2, core), piece(o, 2, core), CORE)
 
-    def rows_end():
-        for o in range(4):
-            for n, dy in ((0, 0), (1, 3), (2, 1), (3, 2)):
-                copies.arrived(ROWC + 4 * o + n, piece(o, dy, other), CORE)
+    def rows_end(o):
+        for n, dy in ((0, 0), (1, 3), (2, 1), (3, 2)):
+            copies.arrived(ROWC + 4 * o + n, piece(o, dy, other), CORE)
 
     TURN, COLZ, COLX = 54, 55, 58
 
@@ -285,61 +289,60 @@
         for d in (1, 2, 3):
             copies.start(COLZ + d - 1, st.at[zlo], st.at[zlo], {"z_lo": up(zlo, d)})
 
-    def cols_z_end():
-        for d in (1, 2, 3):
-            copies.arrived(COLZ + d - 1, st.at[up(zlo, 4 - d)], {"z_lo": up(zlo, d)})
-
     def spot(i, v, s):
         return pc.at[pl.ds(pl.multiple_of((i * 8 + v * 2 + s) * 32, 32), 32)]
 
-    def col_copy(way, h, s, dev):
-        n = COLX + 4 * way + 2 * (h % 2)
+    def col_copy(way, h, dev):
         return pltpu.make_async_remote_copy(
-            src_ref=st.at[h], dst_ref=spot(h % 2, x, s), send_sem=send.at[COLX + 4 * way + h],
-            recv_sem=recv.at[n + s], device_id=dev, device_id_type=MESH,
+            src_ref=st.at[h], dst_ref=spot(lax.rem(h, 2), x, core), send_sem=send.at[COLX + 4 * way + h],
+            recv_sem=recv.at[COLX + 4 * way + 2 * lax.rem(h, 2) + core], device_id=dev, device_id_type=MESH,
         )
 
-    def on_core(s, h, there):
-        n = COLX + 8 + 2 * (h % 2) + s
-        if h // 2 == s:
-            return pltpu.make_async_copy(st.at[h], spot(h % 2, x, s), recv.at[n])
-        return col_copy(2, h, s, {"core": 1 - s})
-
-    def cols_x():
-        for s in (0, 1):
-
-            @pl.when(core == s)
-            def _(s=s):
-                for h in range(4):
-                    for way, dx in ((0, 1), (1, 3)):
-                        col_copy(way, h, s, {"x": up(x, dx), "core": h // 2}).start()
-                    on_core(s, h, None).start()
+    def stay_copy(h):
+        i = lax.rem(h, 2)
+        return pltpu.make_async_copy(st.at[h], spot(i, x, core), recv.at[COLX + 8 + 2 * i + core])
+
+    def cols_x(d):
+        h = up(zlo, 4 - d)
+        to = lax.div(h, 2)
+        if d:
+            copies.arrived(COLZ + d - 1, st.at[h], {"z_lo": up(zlo, d)})
+        for way, dx in ((0, 1), (1, 3)):
+            col_copy(way, h, {"x": up(x, dx), "core": to}).start()
+
+        @pl.when(core == to)
+        def _():
+            stay_copy(h).start()
+
+        @pl.when(core != to)
+        def _():
+            col_copy(2, h, CORE).start()
 
     def cols_x_sent():
-        for s in (0, 1):
-
-            @pl.when(core == s)
-            def _(s=s):
-                for h in range(4):
-                    for way, dx in ((0, 1), (1, 3)):
-                        col_copy(way, h, s, {"x": up(x, dx), "core": h // 2}).wait_send()
-                    if h // 2 != s:
-                        on_core(s, h, None).wait_send()
+        for d in range(4):
+            h = up(zlo, 4 - d)
+            to = lax.div(h, 2)
+            for way, dx in ((0, 1), (1, 3)):
+                col_copy(way, h, {"x": up(x, dx), "core": to}).wait_send()
+
+            @pl.when(core != to)
+            def _():
+                col_copy(2, h, CORE).wait_send()
 
     FAR = COLX + 16
 
-    def cols_forward():
-        for i in (0, 1):
-            for s in (0, 1):
-                copies.arrived(COLX + 2 * i + s, spot(i, up(x, 3), s), X[1])
-                copies.arrived(COLX + 4 + 2 * i + s, spot(i, up(x, 1), s), X[-1])
-            p = spot(i, up(x, 3), 0)
-            copies.start(FAR + 2 * i, p, p, X[1])
-            p = spot(i, up(x, 1), 1)
-            copies.start(FAR + 2 * i + 1, p, p, X[-1])
+    def cols_forward(i):
+        p = spot(i, up(x, 3), 0)
+        copies.arrived(COLX + 2 * i, p, X[1])
+        copies.start(FAR + 2 * i, p, p, X[1])
+        p = spot(i, up(x, 1), 1)
+        copies.arrived(COLX + 4 + 2 * i + 1, p, X[-1])
+        copies.start(FAR + 2 * i + 1, p, p, X[-1])
 
     def cols_end():
         for i in (0, 1):
+            copies.arrived(COLX + 2 * i + 1, spot(i, up(x, 3), 1), X[1])
+            copies.arrived(COLX + 4 + 2 * i, spot(i, up(x, 1), 0), X[-1])
             for s in (0, 1):
                 copies.arrived(COLX + 8 + 2 * i + s, spot(i, x, s), CORE)
                 copies.arrived(FAR + 2 * i + s, spot(i, up(x, 2), s), X[1])
@@ -348,61 +351,67 @@
     diag_z(BD, bd)
     own_b.wait()
     own_a.wait()
-    rows_z()
     turn()
     rows_y(0)
     load_trail.start()
+    eye = lax.broadcasted_iota(jnp.int32, (512, 512), 0) == lax.broadcasted_iota(jnp.int32, (512, 512), 1)
+    aw[:, 512:] = jnp.where(eye, 1.0, 0.0).astype(f32)
     diag_x(BD, bd)
+    diag_forward(BD, bd)
+    turned_here()
+    cols_z()
+    cols_x(0)
+    diag_last(BD, bd)
+    rows_z()
     own_ad.wait()
     diag_z(AD, ad)
-    diag_forward(BD, bd)
-    diag_last(BD, bd)
-    eye = lax.broadcasted_iota(jnp.int32, (512, 512), 0) == lax.broadcasted_iota(jnp.int32, (512, 512), 1)
-    aw[:, 512:] = jnp.where(eye, 1.0, 0.0).astype(f32)
     diag_end(BD, bd)
     aw[:, :512] = bd[...].reshape(512, 512)
 
-    def between(k):
-        if k == 0:
-            turned_here()
-            cols_z()
+    def between(n):
+        if n == 0:
             rows_y_forward(0)
+        if n == 2:
+            rows_y_last(0)
+        if n == 5:
+            cols_x(1)
+        if n == 6:
+            cols_x(3)
+        if n == 7:
+            cols_x(2)
+        if n == 8:
             diag_x(AD, ad)
-        if k == 1:
+        if n == 9:
             rows_z_forward()
             rows_y(1)
             rows_y(2)
-        if k == 2:
-            cols_z_end()
-            cols_x()
-            rows_y_last(0)
+        if n == 11:
             diag_forward(AD, ad)
-        if k == 3:
+        if n == 13:
+            diag_last(AD, ad)
+            rows_z_last()
+            rows_y(3)
+        if n == 14:
             rows_y_forward(1)
             rows_y_forward(2)
-            diag_last(AD, ad)
-        if k == 4:
-            rows_z_last()
-            rows_y(3)
-        if k == 5:
-            rows_y_last(1)
-            rows_y_last(2)
-        if k == 6:
-            rows_y_forward(3)
-        if k == 7:
-            cols_forward()
+        if n == 15:
+            cols_forward(0)
+            cols_forward(1)
 
     invert(aw, between)
     diag_end(AD, ad)
     mid[...] = dot(ad[...].reshape(512, 512), aw[:, 512:], NT)
-    rows_y_last(3)
     w = halves(aw[:, 512:])
+    rows_y_last(1)
+    rows_y_last(2)
     adn[...] = dot(aw[:, 512:], mid[...], NN)
     diag_out[...] = adn[pl.ds(pl.multiple_of(grid_row * 32, 32), 32), :]
     q = halves(adn[...])
+    rows_y_forward(3)
     own_l = dot3(halves(pr[own, 0:512]), w, NT)
     l_out[...] = own_l
     n_out[...] = dot3(halves(pr[own, 512:1024]), w, NT) - dot3(halves(own_l), q, NN)
+    rows_y_last(3)
     cols_end()
     col_l = dot3(halves(pc[:, 0:512]), w, NT)
     lh = halves(col_l)
@@ -412,30 +421,52 @@
     zh[:, 0:512], zl[:, 0:512] = halves(col_z)
     zh[:, 512:1024], zl[:, 512:1024] = halves(col_y)
     load_trail.wait()
-    rows_end()
-
-    def store(t):
-        tile = pl.ds(pl.multiple_of(t * 128, 128), 128)
-        return pltpu.make_async_copy(trail.at[tile], trail_out.at[tile], tout.at[t])
-
-    @pl.loop(0, 8)
-    def _(t):
-        tile = pl.ds(pl.multiple_of(t * 128, 128), 128)
-        trail[tile, :] = trail[tile, :] - dot3(halves(pr[tile, :]), (zh[...], zl[...]), NT)
-        store(t).start()
+
+    def store(o):
+        tile = pl.ds(pl.multiple_of(up(zhi, offsets[o]) * 256, 256), 256)
+        return pltpu.make_async_copy(trail.at[tile], trail_out.at[tile], tout.at[o])
+
+    def update(o):
+        @pl.loop(0, 2)
+        def _(t):
+            tile = pl.ds(pl.multiple_of(up(zhi, offsets[o]) * 256 + t * 128, 128), 128)
+            trail[tile, :] = trail[tile, :] - dot3(halves(pr[tile, :]), (zh[...], zl[...]), NT)
+
+        store(o).start()
+
+    for o in range(4):
+        rows_end(o)
+        update(o)
 
     copies.finish()
     turn_sent()
     cols_x_sent()
-    for t in range(8):
-        store(t).wait()
+    for o in range(4):
+        store(o).wait()
+
+
+def place_results(*refs):
+    ins, outs, (few, many, sems_in, sems_out) = refs[:4], refs[4:8], refs[8:]
+    ways = [(ins[i], few.at[i], outs[i]) for i in range(3)]
+    for t in range(4):
+        rows = pl.ds(256 * t, 256)
+        ways.append((ins[3].at[rows], many.at[rows], outs[3].at[rows]))
+    first = [pltpu.make_async_copy(w[0], w[1], sems_in.at[i]) for i, w in enumerate(ways)]
+    then = [pltpu.make_async_copy(w[1], w[2], sems_out.at[i]) for i, w in enumerate(ways)]
+    for copy in first:
+        copy.start()
+    for i, copy in enumerate(then):
+        first[i].wait()
+        copy.start()
+    for copy in then:
+        copy.wait()
 
 
 def shards(*arrays):
     vmem = pl.BlockSpec(memory_space=pltpu.VMEM)
     anywhere = pl.BlockSpec(memory_space=pl.ANY)
     own = jax.ShapeDtypeStruct((32, 512), f32)
-    return pl.pallas_call(
+    results = pl.pallas_call(
         kernel,
         out_shape=(own, own, own, jax.ShapeDtypeStruct((1024, 512), f32)),
         in_specs=[anywhere] * 5,
@@ -456,11 +487,23 @@
             pltpu.SemaphoreType.DMA((80,)),
             pltpu.SemaphoreType.DMA((4,)),
             pltpu.SemaphoreType.DMA((1,)),
-            pltpu.SemaphoreType.DMA((8,)),
+            pltpu.SemaphoreType.DMA((4,)),
         ],
         compiler_params=pltpu.CompilerParams(collective_id=0, has_side_effects=True, vmem_limit_bytes=56 << 20),
         cost_estimate=pl.CostEstimate(flops=10**10, bytes_accessed=8 << 20, transcendentals=0),
     )(*arrays)
+    return pl.pallas_call(
+        place_results,
+        out_shape=(own, own, own, jax.ShapeDtypeStruct((1024, 512), f32)),
+        in_specs=[anywhere] * 4,
+        out_specs=(anywhere,) * 4,
+        scratch_shapes=[
+            pltpu.VMEM((3, 32, 512), f32),
+            pltpu.VMEM((1024, 512), f32),
+            pltpu.SemaphoreType.DMA((7,)),
+            pltpu.SemaphoreType.DMA((7,)),
+        ],
+    )(*results)
 
 
 def solution(mesh):

time: 116 us -> 98 us (0.84)
  the two profiles are of different devices: /device:TPU:98 before, /device:TPU:24 now
where the time goes in v2:
time: 98 us; the launch traced here: 97.2 us
  Pallas kernels  96.3 us (98%)
    pallas_call x1, Pallas kernels, shards(): pl.pallas_call(kernel, out_shape=(own, own, own, jax.ShapeDtypeStruct((10...  93.7 us
    pallas_call x1, Pallas kernels, shards(): pl.pallas_call(place_results, out_shape=(own, own, own, jax.ShapeDtypeStr...  2.59 us

profile of v2, /device:TPU:24, one launch (start us, length us, event | category | flops | bytes accessed | tf_op | source)
XLA Modules:
  0.0 97.2 jit_solution(1822727011030811036)
XLA Ops:
  0.6 93.7 %shard_map.84 = (f32[32,512]{1,0:T(8,128)}, f32[32,512]{1,0:T(8,128)}, f32[32,512]{1,0:T(8,128)}, f32[1024,512]{1,0:T(8,128)}) custom-call(f32[32,512]{1,0:T(8,128)} %b_diag.1, f32[32,512]{1,0:T(8,128)} %a_diag.1, f32[32,512]{1,0:T(8,128)} %b_panel.1, f32[32,512]{1,0:T(8,128)} %a_panel.1, f32[1024,512]{1,0:T(8,128)} %a_trail.1), custom_call_target="tpu_custom_call" | custom-call | flops 10000000000 | bytes 8388608 | tf_op jit(solution)/shard_map/pallas_call | solution.py:469
  94.4 2.6 %shard_map.85 = (f32[32,512]{1,0:T(8,128)}, f32[32,512]{1,0:T(8,128)}, f32[32,512]{1,0:T(8,128)}, f32[1024,512]{1,0:T(8,128)}) custom-call(f32[32,512]{1,0:T(8,128)} %get-tuple-element.8.refs_0_, f32[32,512]{1,0:T(8,128)} %get-tuple-element.9.refs_1_, f32[32,512]{1,0:T(8,128)} %get-tuple-element.10.refs_2_, f32[1024,512]{1,0:T(8,128)} %get-tuple-element.11.refs_3_), custom_call_target="tpu_custom_call" | custom-call | tf_op jit(solution)/shard_map/pallas_call | solution.py:495

commit v3 on v2

--- a/solution.py
+++ b/solution.py
@@ -30,6 +30,16 @@
         return lax.dot_general(u, v, (dims, ((), ())), preferred_element_type=f32)
 
     return one(a[0], b[0]) + (one(a[0], b[1]) + one(a[1], b[0]))
+
+
+def times_turned(a, w):
+    near = dot3([v[:, 0:256] for v in a], [v[0:256, 0:256] for v in w], NT)
+    return jnp.concatenate([near, dot3(a, [v[256:512] for v in w], NT)], axis=1)
+
+
+def times(a, w):
+    far = dot3([v[:, 256:512] for v in a], [v[256:512, 256:512] for v in w], NN)
+    return jnp.concatenate([dot3(a, [v[:, 0:256] for v in w], NN), far], axis=1)
 
 
 def lane_bcast(x, j):
@@ -400,24 +410,26 @@
 
     invert(aw, between)
     diag_end(AD, ad)
-    mid[...] = dot(ad[...].reshape(512, 512), aw[:, 512:], NT)
     w = halves(aw[:, 512:])
+    mid[...] = times_turned(halves(ad[...].reshape(512, 512)), w)
     rows_y_last(1)
     rows_y_last(2)
-    adn[...] = dot(aw[:, 512:], mid[...], NN)
+    m = halves(mid[...])
+    adn[0:256, :] = dot3([v[0:256, 0:256] for v in w], [v[0:256] for v in m], NN)
+    adn[256:512, :] = dot3([v[256:512] for v in w], m, NN)
     diag_out[...] = adn[pl.ds(pl.multiple_of(grid_row * 32, 32), 32), :]
     q = halves(adn[...])
     rows_y_forward(3)
-    own_l = dot3(halves(pr[own, 0:512]), w, NT)
+    own_l = times_turned(halves(pr[own, 0:512]), w)
     l_out[...] = own_l
-    n_out[...] = dot3(halves(pr[own, 512:1024]), w, NT) - dot3(halves(own_l), q, NN)
+    n_out[...] = times_turned(halves(pr[own, 512:1024]), w) - dot3(halves(own_l), q, NN)
     rows_y_last(3)
     cols_end()
-    col_l = dot3(halves(pc[:, 0:512]), w, NT)
+    col_l = times_turned(halves(pc[:, 0:512]), w)
     lh = halves(col_l)
-    col_n = dot3(halves(pc[:, 512:1024]), w, NT) - dot3(lh, q, NN)
-    col_y = dot3(lh, w, NN)
-    col_z = dot3(halves(col_n), w, NN)
+    col_n = times_turned(halves(pc[:, 512:1024]), w) - dot3(lh, q, NN)
+    col_y = times(lh, w)
+    col_z = times(halves(col_n), w)
     zh[:, 0:512], zl[:, 0:512] = halves(col_z)
     zh[:, 512:1024], zl[:, 512:1024] = halves(col_y)
     load_trail.wait()

time: 98 us -> 96.9 us (0.989)
  Pallas kernels: 96.3 us -> 95 us
    pallas_call x1, Pallas kernels: 93.7 us -> 92.4 us  [shards(): pl.pallas_call(kernel, out_shape=(own, own, own, jax.ShapeDtypeStruct((10...]
where the time goes in v3:
time: 96.9 us; the launch traced here: 95.8 us
  Pallas kernels  95 us (98%)
    pallas_call x1, Pallas kernels, shards(): pl.pallas_call(kernel, out_shape=(own, own, own, jax.ShapeDtypeStruct((10...  92.4 us
    pallas_call x1, Pallas kernels, shards(): pl.pallas_call(place_results, out_shape=(own, own, own, jax.ShapeDtypeStr...  2.59 us

profile of v3, /device:TPU:24, one launch (start us, length us, event | category | flops | bytes accessed | tf_op | source)
XLA Modules:
  0.0 95.8 jit_solution(14121283466099013987)
XLA Ops:
  0.6 92.4 %shard_map.84 = (f32[32,512]{1,0:T(8,128)}, f32[32,512]{1,0:T(8,128)}, f32[32,512]{1,0:T(8,128)}, f32[1024,512]{1,0:T(8,128)}) custom-call(f32[32,512]{1,0:T(8,128)} %b_diag.1, f32[32,512]{1,0:T(8,128)} %a_diag.1, f32[32,512]{1,0:T(8,128)} %b_panel.1, f32[32,512]{1,0:T(8,128)} %a_panel.1, f32[1024,512]{1,0:T(8,128)} %a_trail.1), custom_call_target="tpu_custom_call" | custom-call | flops 10000000000 | bytes 8388608 | tf_op jit(solution)/shard_map/pallas_call | solution.py:481
  93.0 2.6 %shard_map.85 = (f32[32,512]{1,0:T(8,128)}, f32[32,512]{1,0:T(8,128)}, f32[32,512]{1,0:T(8,128)}, f32[1024,512]{1,0:T(8,128)}) custom-call(f32[32,512]{1,0:T(8,128)} %get-tuple-element.8.refs_0_, f32[32,512]{1,0:T(8,128)} %get-tuple-element.9.refs_1_, f32[32,512]{1,0:T(8,128)} %get-tuple-element.10.refs_2_, f32[1024,512]{1,0:T(8,128)} %get-tuple-element.11.refs_3_), custom_call_target="tpu_custom_call" | custom-call | tf_op jit(solution)/shard_map/pallas_call | solution.py:507
